TPU v7x, 32 devices: a whole 2x2x4 slice. The times are simulated.
32 devices in a mesh: shot: 2 (over y), gx: 4 (over z), sec: 2 (over x), gy: 2 (over core).
Axes of the slice: x: 2, y: 2, z: 4, core: 2. Of those that a mesh axis runs over, the one named last changes fastest.
Arguments:
- source_fields: float32 [8, 16, 32, 256], P('shot', 'sec', 'gx', 'gy'), parts along dimension 0, may hold values from -6 to 6
- receiver_fields: float32 [8, 16, 32, 256], P('shot', 'sec', 'gx', 'gy'), parts along dimension 0, may hold values from -6 to 6
- courant: float32 [16, 32, 256], P('sec', 'gx', 'gy'), may hold values from 0.05 to 0.15
- epsilon: float32 [16, 32, 256], P('sec', 'gx', 'gy'), may hold values from 0.05 to 0.3
- delta_param: float32 [16, 32, 256], P('sec', 'gx', 'gy'), may hold values from 0 to 0.15
- tilt_angle: float32 [16, 32, 256], P('sec', 'gx', 'gy'), may hold values from -0.8 to 0.8
- source_pos: int32 [6], P('shot'), parts along dimension 0, may hold values from 0 to 255, as said below
- wavelet: float32 [18], P('shot'), parts along dimension 0, may hold values from -24 to 24
- receiver_pos: int32 [512, 3], P('shot'), parts along dimension 0, may hold values from 0 to 255, as said below
- receiver_data: float32 [18, 256], P('shot'), parts along dimension 0, may hold values from -6 to 6
- step_counts: int32 [3], replicated, may hold values from 1 to 3, as said below
- offset_lags: int32 [48, 2], replicated, may hold values from -8 to 8, as said below
Outputs:
- offset_images: bfloat16 [96, 16, 32, 256], P('shot', 'sec', 'gx', 'gy'), parts along dimension 0
- source_out: float32 [8, 16, 32, 256], P('shot', 'sec', 'gx', 'gy'), parts along dimension 0
- receiver_out: float32 [8, 16, 32, 256], P('shot', 'sec', 'gx', 'gy'), parts along dimension 0
There are 2 independent parts, one for each index of `shot`. A program takes and returns all parts, laid end to end along the dimension named above; an argument that names none is the same for every part. Nothing has to cross between parts.
Inputs may be any that keep to these rules, and one draw needn't show every extreme that they name: `source_pos`: a grid cell: depth below 16, first horizontal below 32, second horizontal below 256; it lies on the last cell of the longest grid dimension and on cell 0 of another dimension. `receiver_pos`: grid cells: depth below 16, first horizontal below 32, second horizontal below 256; one receiver sits at the far corner of the grid and one at its anchor. `step_counts`: some snapshot takes all 3 steps. `offset_lags`: in each dimension some lag is 8 and some is minus 8.
All inputs are finite; a program needn't handle non-finite values.
Results may differ from a plain program's by a relative error of at most 0.001.
The roundings to bfloat16 on the way count: a program that leaves them out, or rounds other values in their place, can miss the bound.
Values may be sent and summed in bfloat16 or wider, within the bound.
A program may use at most 64 MiB of HBM per device.

v0:
```python
import functools

import jax
import jax.numpy as jnp
from jax import lax
from jax.experimental import pallas as pl
from jax.experimental.pallas import tpu as pltpu
from jax.sharding import PartitionSpec as P

SNAPS = 3
STEPS = 3
DEEP = STEPS
MESH = pl.DeviceIdType.MESH

TOP = 8
SIDE = 4
WAYS = ((-1, 0), (1, 0), (0, -1), (0, 1), (-1, -1), (-1, 1), (1, -1), (1, 1))
SNAP_WAYS = ((-1, False), (1, False), (0, True), (-1, True), (1, True))


def layers(dx, dz, depth, nz, nx):
    if dz == 0:
        z_from, z_to, z_count = DEEP, DEEP, nz
    elif dz < 0:
        z_from, z_to, z_count = DEEP, DEEP + nz, depth
    else:
        z_from, z_to, z_count = DEEP + nz - depth, DEEP - depth, depth
    first = TOP + SIDE
    if dx == 0:
        x_from, x_to, x_count = first, first, nx
    elif dx < 0:
        x_from, x_to, x_count = first, first + nx, depth
    else:
        x_from, x_to, x_count = first + nx - depth, first - depth, depth
    return z_from, z_to, z_count, x_from, x_to, x_count


def message_rows(dx, dz, depths, nz, nx):
    total = 0
    for depth in depths:
        _, _, z_count, _, _, x_count = layers(dx, dz, depth, nz, nx)
        total += z_count * x_count
    return -(-total // 8) * 8


FIELD_DEPTHS = (DEEP, DEEP, DEEP - 1, DEEP - 1)
COEF_DEPTHS = (DEEP - 1,) * 4


def kernel(
    sizes,
    src_ref,
    rec_ref,
    cou_ref,
    eps_ref,
    del_ref,
    tilt_ref,
    spos_ref,
    wav_ref,
    rpos_ref,
    rdat_ref,
    cnt_ref,
    lag_ref,
    img_ref,
    so_ref,
    ro_ref,
    *scratch,
):
    small_hbm = (spos_ref, wav_ref, cnt_ref, lag_ref, rpos_ref, rdat_ref)
    small = scratch[-6:]
    spos_ref, wav_ref, cnt_ref, lag_ref, rpos_ref, rdat_ref = small
    scratch = scratch[:-6]
    now, new, old, raw, coef, dep = scratch[:6]
    mine, theirs, halves = scratch[6:9]
    field_send, field_recv = scratch[9:17], scratch[17:25]
    coef_send, coef_recv = scratch[25:33], scratch[33:41]
    snap_send, snap_recv, centre, beside, acc, both, give = scratch[41:48]
    load_sem, pair_ssem, pair_rsem, halo_ssem, halo_rsem, snap_ssem, snap_rsem = scratch[48:]
    nz, nx, ny = cou_ref.shape
    nlag = lag_ref.shape[1]
    window = nx + 2 * SIDE
    first = TOP + SIDE
    rows = slice(TOP, TOP + window)
    block = slice(first, first + nx)
    ngx, nsec, _ = sizes
    gx, sec, gy = lax.axis_index("gx"), lax.axis_index("sec"), lax.axis_index("gy")
    is_source = gy == 0

    def exists(dx, dz):
        ok = None
        if dx:
            ok = gx > 0 if dx < 0 else gx < ngx - 1
        if dz:
            okz = sec > 0 if dz < 0 else sec < nsec - 1
            ok = okz if ok is None else jnp.logical_and(ok, okz)
        return ok

    def guarded(ok, action):
        if ok is None:
            action()
        else:
            pl.when(ok)(action)

    def device(dx, dz, other):
        where = {}
        if dx:
            where["gx"] = gx + dx
        if dz:
            where["sec"] = sec + dz
        if other:
            where["gy"] = 1 - gy
        return where

    def remote(src, dst, send_sem, recv_sem, where):
        return pltpu.make_async_remote_copy(
            src_ref=src,
            dst_ref=dst,
            send_sem=send_sem,
            recv_sem=recv_sem,
            device_id=where,
            device_id_type=MESH,
        )

    coef_refs = (cou_ref, eps_ref, del_ref, tilt_ref)
    loads = [
        pltpu.make_async_copy(ref, halves.at[0, i], load_sem.at[i])
        for i, ref in enumerate(coef_refs)
    ]
    loads += [
        pltpu.make_async_copy(ref, held, load_sem.at[5 + i])
        for i, (ref, held) in enumerate(zip(small_hbm, small))
    ]
    for copy in loads:
        copy.start()
    load_source = pltpu.make_async_copy(src_ref, mine, load_sem.at[4])
    load_receiver = pltpu.make_async_copy(rec_ref, mine, load_sem.at[4])
    pl.when(is_source)(load_source.start)
    pl.when(jnp.logical_not(is_source))(load_receiver.start)

    barrier = pltpu.get_barrier_semaphore()
    total = jnp.int32(1)
    pl.semaphore_signal(barrier, inc=1, device_id=device(0, 0, True), device_id_type=MESH)
    for dx, dz, other in [(dx, dz, False) for dx, dz in WAYS] + [(-1, 0, True), (1, 0, True)]:
        ok = exists(dx, dz)
        total = total + ok.astype(jnp.int32)

        @pl.when(ok)
        def _():
            pl.semaphore_signal(
                barrier, inc=1, device_id=device(dx, dz, other), device_id_type=MESH
            )

    for ref in (now, old, raw):
        ref[:, :, :, rows, :] = jnp.zeros(ref.shape[:3] + (window, ny), jnp.float32)
    centre[...] = jnp.zeros_like(centre)
    beside[...] = jnp.zeros_like(beside)
    pl.semaphore_wait(barrier, total)

    pairs = [
        remote(ref, halves.at[1, i], pair_ssem.at[i], pair_rsem.at[i], device(0, 0, True))
        for i, ref in enumerate(coef_refs)
    ]
    to_pair = device(0, 0, True)
    swap_receiver = remote(rec_ref, theirs, pair_ssem.at[4], pair_rsem.at[4], to_pair)
    swap_source = remote(src_ref, theirs, pair_ssem.at[4], pair_rsem.at[4], to_pair)
    for copy in pairs:
        copy.start()
    pl.when(is_source)(swap_receiver.start)
    pl.when(jnp.logical_not(is_source))(swap_source.start)

    def joined(own, other):
        left = jnp.where(is_source, own, other)
        right = jnp.where(is_source, other, own)
        return left, right

    def split(left, right):
        return jnp.where(is_source, left, right), jnp.where(is_source, right, left)

    def pack(buffer, arrays, depths, dx, dz):
        at = 0
        for (ref, f), depth in zip(arrays, depths):
            z_from, _, z_count, x_from, _, x_count = layers(dx, dz, depth, nz, nx)
            for z in range(z_count):
                buffer[:, at : at + x_count, :] = ref[f, z_from + z, :, x_from : x_from + x_count, :]
                at += x_count

    def unpack(buffer, arrays, depths, dx, dz):
        at = 0
        for (ref, f), depth in zip(arrays, depths):
            _, z_to, z_count, _, x_to, x_count = layers(dx, dz, depth, nz, nx)
            for z in range(z_count):
                ref[f, z_to + z, :, x_to : x_to + x_count, :] = buffer[:, at : at + x_count, :]
                at += x_count

    coef_arrays = [(raw, i) for i in range(4)]
    field_arrays = [(now, 0), (now, 1), (old, 0), (old, 1)]

    def coef_copy(n):
        return remote(
            coef_send[n],
            coef_recv[n],
            halo_ssem.at[SNAPS, n],
            halo_rsem.at[SNAPS, n],
            device(*WAYS[n], False),
        )

    def field_copy(s, n):
        return remote(
            field_send[n].at[s],
            field_recv[n].at[s],
            halo_ssem.at[s, n],
            halo_rsem.at[s, n],
            device(*WAYS[n], False),
        )

    def send_fields(s):
        for n, (dx, dz) in enumerate(WAYS):

            def go():
                pack(field_send[n].at[s], field_arrays, FIELD_DEPTHS, dx, dz)
                field_copy(s, n).start()

            guarded(exists(dx, dz), go)

    def take_fields(s):
        for n, (dx, dz) in enumerate(WAYS):

            def go():
                field_copy(s, n).wait_recv()
                unpack(field_recv[n].at[s], field_arrays, FIELD_DEPTHS, dx, dz)

            guarded(exists(-dx, -dz), go)

    for copy in loads:
        copy.wait()
    load_source.wait()
    for copy in pairs:
        copy.wait_recv()
    swap_source.wait_recv()
    for ref, f, own, other in [
        (raw, i, halves.at[0, i], halves.at[1, i]) for i in range(4)
    ] + [(ref, f, mine.at[i], theirs.at[i]) for i, (ref, f) in enumerate(field_arrays)]:
        left, right = joined(own[...], other[...])
        ref[f, DEEP : DEEP + nz, 0, block, :] = left
        ref[f, DEEP : DEEP + nz, 1, block, :] = right

    for n, (dx, dz) in enumerate(WAYS):

        def go():
            pack(coef_send[n], coef_arrays, COEF_DEPTHS, dx, dz)
            coef_copy(n).start()

        guarded(exists(dx, dz), go)

    planes = nz + 2 * (DEEP - 1)

    def deposits(s):
        nrec = rpos_ref.shape[1]
        lane = lax.broadcasted_iota(jnp.int32, (1, nrec), 1)

        def points(d):
            alone = jnp.where(lane == 0, spos_ref[d], -1)
            return jnp.where(is_source, alone, rpos_ref[d : d + 1, :])

        pz = points(0) - sec * nz + (DEEP - 1)
        px = points(1) - gx * nx + SIDE
        py = points(2)
        at_y = lax.broadcasted_iota(jnp.int32, (2 * ny, nrec), 0) == py
        at_y = jnp.where(at_y, 1.0, 0.0).astype(jnp.bfloat16)
        cell = jnp.where((px >= 0) & (px < window), pz * window + px, -1)
        at_cell = lax.broadcasted_iota(jnp.int32, (planes * window, nrec), 0) == cell
        for j in range(STEPS):
            t = s * STEPS + j
            alone = jnp.where(lane == 0, wav_ref[t], 0.0)
            amounts = jnp.where(is_source, alone, rdat_ref[pl.ds(t, 1), :])
            high = amounts.astype(jnp.bfloat16).astype(jnp.float32)
            summed = None
            for part in (high, amounts - high):
                picked = jnp.where(at_cell, part, 0.0).astype(jnp.bfloat16)
                term = lax.dot_general(
                    picked, at_y, (((1,), (1,)), ((), ())), preferred_element_type=jnp.float32
                )
                summed = term if summed is None else summed + term
            for half in range(2):
                lanes = summed[:, half * ny : (half + 1) * ny]
                dep[j, :, half] = lanes.reshape(planes, window, ny)

    def coefficients():
        for n, (dx, dz) in enumerate(WAYS):

            def go():
                coef_copy(n).wait_recv()
                unpack(coef_recv[n], coef_arrays, COEF_DEPTHS, dx, dz)

            guarded(exists(-dx, -dz), go)

        def plane(z, carry):
            tilt = raw[3, 1 + z, :, rows, :]
            cos_tilt, sin_tilt = jnp.cos(tilt), jnp.sin(tilt)
            coef[0, z] = raw[0, 1 + z, :, rows, :]
            coef[1, z] = 1.0 + 2.0 * raw[1, 1 + z, :, rows, :]
            coef[2, z] = 1.0 + 2.0 * raw[2, 1 + z, :, rows, :]
            coef[3, z] = cos_tilt * cos_tilt
            coef[4, z] = sin_tilt * sin_tilt
            coef[5, z] = 0.5 * sin_tilt * cos_tilt
            return carry

        lax.fori_loop(0, planes, plane, 0)

    def snap_copy(s, n):
        dx, other = SNAP_WAYS[n]
        return remote(
            snap_send.at[s],
            snap_recv.at[s, n],
            snap_ssem.at[s, n],
            snap_rsem.at[s, n],
            device(dx, 0, other),
        )

    lane = lax.broadcasted_iota(jnp.int32, (nx, ny), 1)
    keep = (lane < ny // 2) == is_source

    def place(s, section, dx, whole):
        start = nx - dx * nx
        whole = whole.astype(jnp.float32)
        own, other = split(whole[0].reshape(nz, nx, ny), whole[1].reshape(nz, nx, ny))
        centre[s, section, :, start : start + nx, :] = own
        beside[s, section, :, start : start + nx, :] = jnp.where(keep[None], other, 0.0)

    def send_snapshot(s, ref):
        for half in range(2):
            rounded = ref[0, DEEP : DEEP + nz, half, block, :].astype(jnp.bfloat16)
            snap_send[s, half] = rounded.reshape(nz * nx, ny)
        for n, (dx, other) in enumerate(SNAP_WAYS):
            guarded(exists(dx, 0), snap_copy(s, n).start)
        place(s, gy, 0, snap_send[s])

    def take_snapshot(s):
        for n, (dx, other) in enumerate(SNAP_WAYS):

            def go():
                snap_copy(s, n).wait_recv()
                place(s, 1 - gy if other else gy, dx, snap_recv[s, n])

            guarded(exists(-dx, 0), go)

    def image(s):
        def one_lag(lag, carry):
            lx = lag_ref[0, lag]
            ly = lag_ref[1, lag]

            def shifted(h, sx, sy):
                c = centre[s, h, :, pl.ds(nx + sx, nx), :]
                b = beside[s, h, :, pl.ds(nx + sx, nx), :]
                edge = jnp.logical_or(lane < sy, lane >= ny + sy)
                mixed = jnp.where(edge[None], b, c)
                return pltpu.roll(mixed, lax.rem(ny - sy, ny), 2)

            product = shifted(0, -lx, -ly) * shifted(1, lx, ly)
            product = product.reshape(nz * nx, ny)
            if s == 0:
                acc[lag] = product
            elif s < SNAPS - 1:
                acc[lag] = acc[lag] + product
            else:
                img_ref[lag] = (acc[lag] + product).astype(jnp.bfloat16)
            return carry

        some = 4 if nlag % 4 == 0 else 1

        def lags(i, carry):
            for more in range(some):
                one_lag(i * some + more, carry)
            return carry

        lax.fori_loop(0, nlag // some, lags, 0)

    step_lane = lax.broadcasted_iota(jnp.int32, (window, ny), 1)
    first_lane = step_lane == 0
    last_lane = step_lane == ny - 1

    def advance(j, halo, active, here, there):
        for z in range(DEEP - halo, DEEP + nz + halo):
            c = z - 1
            left, right = here[0, z, 0, rows, :], here[0, z, 1, rows, :]
            left_up, right_up = pltpu.roll(left, ny - 1, 1), pltpu.roll(right, ny - 1, 1)
            left_down, right_down = pltpu.roll(left, 1, 1), pltpu.roll(right, 1, 1)
            sides = (
                jnp.where(last_lane, right_up, left_up) + jnp.where(first_lane, 0.0, left_down),
                jnp.where(last_lane, 0.0, right_up) + jnp.where(first_lane, left_down, right_down),
            )
            for half in range(2):

                def diffs(f):
                    def at(dz, dx):
                        return here[f, z + dz, half, TOP + dx : TOP + window + dx, :]

                    mid = at(0, 0)
                    twice = 2.0 * mid
                    zz = at(1, 0) + at(-1, 0) - twice
                    xx = at(0, 1) + at(0, -1) - twice
                    xz = at(1, 1) - at(1, -1) - at(-1, 1) + at(-1, -1)
                    return mid, twice, zz, xx, xz

                p, twice_p, pzz, pxx, pxz = diffs(0)
                q, twice_q, qzz, qxx, qxz = diffs(1)
                pyy = sides[half] - twice_p
                wz, wx, wm = coef[3, c, half], coef[4, c, half], coef[5, c, half]
                vert_p = wz * pzz + wx * pxx + wm * pxz
                horiz = pzz + pxx + pyy - vert_p
                vert_q = wz * qzz + wx * qxx + wm * qxz
                p_old, q_old = old[0, z, half, rows, :], old[1, z, half, rows, :]
                amount = dep[j, c, half]
                cou = coef[0, c, half]
                new_p = twice_p - p_old + cou * (coef[1, c, half] * horiz + vert_q) + amount
                new_q = twice_q - q_old + cou * (coef[2, c, half] * horiz + vert_q) + amount
                there[0, z, half, rows, :] = jnp.where(active, new_p, p)
                there[1, z, half, rows, :] = jnp.where(active, new_q, q)
                old[0, z, half, rows, :] = jnp.where(active, p, p_old)
                old[1, z, half, rows, :] = jnp.where(active, q, q_old)

    def window_steps(s, carry):
        send_fields(s)

        @pl.when(s > 0)
        def _():
            send_snapshot(s - 1, now)

        deposits(s)
        pl.when(s == 0)(coefficients)

        @pl.when(s == SNAPS - 1)
        def _():
            take_snapshot(0)
            image(0)

        take_fields(s)
        here, there = now, new
        for j in range(STEPS):
            advance(j, STEPS - 1 - j, j < cnt_ref[s], here, there)
            here, there = there, here
        if here is new:
            for f in range(2):
                now[f, DEEP : DEEP + nz, :, rows, :] = new[f, DEEP : DEEP + nz, :, rows, :]
        return carry

    lax.fori_loop(0, SNAPS, window_steps, 0)

    send_snapshot(SNAPS - 1, now)
    for i, (ref, f) in enumerate(field_arrays):
        own, other = split(
            ref[f, DEEP : DEEP + nz, 0, block, :], ref[f, DEEP : DEEP + nz, 1, block, :]
        )
        both[gy, i] = own
        give[i] = other
    back = remote(give, both.at[gy], pair_ssem.at[5], pair_rsem.at[5], to_pair)
    back.start()
    for s in range(1, SNAPS - 1):
        take_snapshot(s)
        image(s)
    take_snapshot(SNAPS - 1)
    image(SNAPS - 1)
    remote(give, both.at[1 - gy], pair_ssem.at[5], pair_rsem.at[5], to_pair).wait_recv()
    so_ref[...] = both[0]
    ro_ref[...] = both[1]

    back.wait_send()
    for copy in pairs:
        copy.wait_send()
    swap_source.wait_send()
    for n, (dx, dz) in enumerate(WAYS):

        def ended():
            coef_copy(n).wait_send()
            for s in range(SNAPS):
                field_copy(s, n).wait_send()

        guarded(exists(dx, dz), ended)
    for n, (dx, _) in enumerate(SNAP_WAYS):

        def ended():
            for s in range(SNAPS):
                snap_copy(s, n).wait_send()

        guarded(exists(dx, 0), ended)


def local(
    sizes,
    source_fields,
    receiver_fields,
    courant,
    epsilon,
    delta_param,
    tilt_angle,
    source_pos,
    wavelet,
    receiver_pos,
    receiver_data,
    step_counts,
    offset_lags,
):
    nz, nx, ny = courant.shape
    nlag = offset_lags.shape[0]
    f32, bf16 = jnp.float32, jnp.bfloat16
    vmem = pl.BlockSpec(memory_space=pltpu.VMEM)
    hbm = pl.BlockSpec(memory_space=pltpu.HBM)
    window = nx + 2 * SIDE
    whole = (nz + 2 * DEEP, 2, window + 2 * TOP, ny)
    inner = (nz + 2 * (DEEP - 1), 2, window, ny)
    field_rows = [message_rows(dx, dz, FIELD_DEPTHS, nz, nx) for dx, dz in WAYS]
    coef_rows = [message_rows(dx, dz, COEF_DEPTHS, nz, nx) for dx, dz in WAYS]
    images, source_out, receiver_out = pl.pallas_call(
        functools.partial(kernel, sizes),
        out_shape=(
            jax.ShapeDtypeStruct((nlag, nz * nx, ny), bf16),
            jax.ShapeDtypeStruct(source_fields.shape, f32),
            jax.ShapeDtypeStruct(receiver_fields.shape, f32),
        ),
        in_specs=[hbm] * 12,
        out_specs=(vmem, vmem, vmem),
        scratch_shapes=[
            pltpu.VMEM((2, *whole), f32),
            pltpu.VMEM((2, *whole), f32),
            pltpu.VMEM((2, *whole), f32),
            pltpu.VMEM((4, *whole), f32),
            pltpu.VMEM((6, *inner), f32),
            pltpu.VMEM((STEPS, *inner), f32),
            pltpu.VMEM((4, nz, nx, ny), f32),
            pltpu.VMEM((4, nz, nx, ny), f32),
            pltpu.VMEM((2, 4, nz, nx, ny), f32),
            *[pltpu.VMEM((SNAPS, 2, count, ny), f32) for count in field_rows * 2],
            *[pltpu.VMEM((2, count, ny), f32) for count in coef_rows * 2],
            pltpu.VMEM((SNAPS, 2, nz * nx, ny), bf16),
            pltpu.VMEM((SNAPS, len(SNAP_WAYS), 2, nz * nx, ny), bf16),
            pltpu.VMEM((SNAPS, 2, nz, 3 * nx, ny), f32),
            pltpu.VMEM((SNAPS, 2, nz, 3 * nx, ny), f32),
            pltpu.VMEM((nlag, nz * nx, ny), f32),
            pltpu.VMEM((2, 4, nz, nx, ny), f32),
            pltpu.VMEM((4, nz, nx, ny), f32),
            pltpu.SemaphoreType.DMA((11,)),
            pltpu.SemaphoreType.DMA((6,)),
            pltpu.SemaphoreType.DMA((6,)),
            pltpu.SemaphoreType.DMA((SNAPS + 1, len(WAYS))),
            pltpu.SemaphoreType.DMA((SNAPS + 1, len(WAYS))),
            pltpu.SemaphoreType.DMA((SNAPS, len(SNAP_WAYS))),
            pltpu.SemaphoreType.DMA((SNAPS, len(SNAP_WAYS))),
            pltpu.SMEM(source_pos.shape, jnp.int32),
            pltpu.SMEM(wavelet.shape, f32),
            pltpu.SMEM(step_counts.shape, jnp.int32),
            pltpu.SMEM(offset_lags.shape[::-1], jnp.int32),
            pltpu.VMEM(receiver_pos.shape[::-1], jnp.int32),
            pltpu.VMEM(receiver_data.shape, f32),
        ],
        compiler_params=pltpu.CompilerParams(
            collective_id=0, has_side_effects=True, vmem_limit_bytes=48 * 1024 * 1024
        ),
    )(
        *(
            pltpu.with_memory_space_constraint(x, pltpu.HBM)
            for x in (
                source_fields,
                receiver_fields,
                courant,
                epsilon,
                delta_param,
                tilt_angle,
                source_pos,
                wavelet,
                receiver_pos.T,
                receiver_data,
                step_counts,
                offset_lags.T,
            )
        )
    )
    return images.reshape(nlag, nz, nx, ny), source_out, receiver_out


def solution(mesh):
    fields = P("shot", "sec", "gx", "gy")
    grid = P("sec", "gx", "gy")
    sizes = tuple(mesh.shape[axis] for axis in ("gx", "sec", "gy"))
    return jax.shard_map(
        functools.partial(local, sizes),
        mesh=mesh,
        in_specs=(
            fields,
            fields,
            grid,
            grid,
            grid,
            grid,
            P("shot"),
            P("shot"),
            P("shot", None),
            P("shot", None),
            P(),
            P(),
        ),
        out_specs=(fields, fields, fields),
        check_vma=False,
    )
```

profile of v0, /device:TPU:0, one launch (start us, length us, event | category | flops | bytes accessed | tf_op | source)
XLA Modules:
  0.0 35.3 jit_solution(18226196017292315835)
XLA Ops:
  0.6 32.4 %shard_map.139 = (bf16[48,64,128]{2,1,0:T(8,128)(2,1)S(1)}, f32[4,8,8,128]{3,2,1,0:T(8,128)S(1)}, f32[4,8,8,128]{3,2,1,0:T(8,128)S(1)}) custom-call(f32[4,8,8,128]{3,2,1,0:T(8,128)} %src_ref.1, f32[4,8,8,128]{3,2,1,0:T(8,128)} %rec_ref.1, f32[8,8,128]{2,1,0:T(8,128)} %cou_ref.1, f32[8,8,128]{2,1,0:T(8,128)} %eps_ref.1, f32[8,8,128]{2,1,0:T(8,128)} %del_ref.1, ...), custom_call_target="tpu_custom_call" | custom-call | tf_op jit(solution)/shard_map/pallas_call | solution.py:513
  33.1 0.9 %copy.18 = bf16[48,8,8,128]{3,2,1,0:T(8,128)(2,1)} copy(bf16[48,8,8,128]{3,2,1,0:T(8,128)(2,1)S(1)} %bitcast.3) | data formatting | bytes 1572864
  34.0 0.7 %copy.19 = f32[4,8,8,128]{3,2,1,0:T(8,128)} copy(f32[4,8,8,128]{3,2,1,0:T(8,128)S(1)} %get-tuple-element.13) | data formatting | bytes 262144
  34.6 0.7 %copy.20 = f32[4,8,8,128]{3,2,1,0:T(8,128)} copy(f32[4,8,8,128]{3,2,1,0:T(8,128)S(1)} %get-tuple-element.14) | data formatting | bytes 262144
where the time goes:
time: 35.4 us; the launch traced here: 35.3 us
  Pallas kernels  32.4 us (92%)
  local copies, waits for them, and re-layouts  2.19 us (6%)
  between operations  0.64 us (2%)
    pallas_call x1, Pallas kernels, local(): pl.pallas_call(functools.partial(kernel, sizes), out_shape=(jax.ShapeDtyp...  32.4 us
    unnamed x3, local copies, waits for them, and re-layouts  2.19 us

commit v1 on v0

--- a/solution.py
+++ b/solution.py
@@ -180,17 +180,23 @@
         at = 0
         for (ref, f), depth in zip(arrays, depths):
             z_from, _, z_count, x_from, _, x_count = layers(dx, dz, depth, nz, nx)
-            for z in range(z_count):
-                buffer[:, at : at + x_count, :] = ref[f, z_from + z, :, x_from : x_from + x_count, :]
+            chunks = [
+                ref[f, z_from + z, :, x_from : x_from + x_count, :] for z in range(z_count)
+            ]
+            for chunk in chunks:
+                buffer[:, at : at + x_count, :] = chunk
                 at += x_count
 
     def unpack(buffer, arrays, depths, dx, dz):
         at = 0
         for (ref, f), depth in zip(arrays, depths):
             _, z_to, z_count, _, x_to, x_count = layers(dx, dz, depth, nz, nx)
+            chunks = []
             for z in range(z_count):
-                ref[f, z_to + z, :, x_to : x_to + x_count, :] = buffer[:, at : at + x_count, :]
+                chunks.append(buffer[:, at : at + x_count, :])
                 at += x_count
+            for z, chunk in enumerate(chunks):
+                ref[f, z_to + z, :, x_to : x_to + x_count, :] = chunk
 
     coef_arrays = [(raw, i) for i in range(4)]
     field_arrays = [(now, 0), (now, 1), (old, 0), (old, 1)]
@@ -345,7 +351,9 @@
             guarded(exists(-dx, 0), go)
 
     def image(s):
-        def one_lag(lag, carry):
+        some = 4 if nlag % 4 == 0 else 1
+
+        def product(lag):
             lx = lag_ref[0, lag]
             ly = lag_ref[1, lag]
 
@@ -356,30 +364,29 @@
                 mixed = jnp.where(edge[None], b, c)
                 return pltpu.roll(mixed, lax.rem(ny - sy, ny), 2)
 
-            product = shifted(0, -lx, -ly) * shifted(1, lx, ly)
-            product = product.reshape(nz * nx, ny)
-            if s == 0:
-                acc[lag] = product
-            elif s < SNAPS - 1:
-                acc[lag] = acc[lag] + product
-            else:
-                img_ref[lag] = (acc[lag] + product).astype(jnp.bfloat16)
+            term = shifted(0, -lx, -ly) * shifted(1, lx, ly)
+            term = term.reshape(nz * nx, ny)
+            return term if s == 0 else acc[lag] + term
+
+        def lags(i, carry):
+            terms = [product(i * some + more) for more in range(some)]
+            for more, term in enumerate(terms):
+                if s < SNAPS - 1:
+                    acc[i * some + more] = term
+                else:
+                    img_ref[i * some + more] = term.astype(jnp.bfloat16)
             return carry
 
-        some = 4 if nlag % 4 == 0 else 1
-
-        def lags(i, carry):
-            for more in range(some):
-                one_lag(i * some + more, carry)
-            return carry
-
         lax.fori_loop(0, nlag // some, lags, 0)
 
-    step_lane = lax.broadcasted_iota(jnp.int32, (window, ny), 1)
-    first_lane = step_lane == 0
-    last_lane = step_lane == ny - 1
-
     def advance(j, halo, active, here, there):
+        skip = SIDE if halo == 0 else 0
+        start, stop = TOP + skip, TOP + window - skip
+        rows = slice(start, stop)
+        inner = slice(skip, window - skip)
+        step_lane = lax.broadcasted_iota(jnp.int32, (stop - start, ny), 1)
+        first_lane = step_lane == 0
+        last_lane = step_lane == ny - 1
         for z in range(DEEP - halo, DEEP + nz + halo):
             c = z - 1
             left, right = here[0, z, 0, rows, :], here[0, z, 1, rows, :]
@@ -393,7 +400,7 @@
 
                 def diffs(f):
                     def at(dz, dx):
-                        return here[f, z + dz, half, TOP + dx : TOP + window + dx, :]
+                        return here[f, z + dz, half, start + dx : stop + dx, :]
 
                     mid = at(0, 0)
                     twice = 2.0 * mid
@@ -405,15 +412,15 @@
                 p, twice_p, pzz, pxx, pxz = diffs(0)
                 q, twice_q, qzz, qxx, qxz = diffs(1)
                 pyy = sides[half] - twice_p
-                wz, wx, wm = coef[3, c, half], coef[4, c, half], coef[5, c, half]
+                wz, wx, wm = (coef[i, c, half, inner, :] for i in (3, 4, 5))
                 vert_p = wz * pzz + wx * pxx + wm * pxz
                 horiz = pzz + pxx + pyy - vert_p
                 vert_q = wz * qzz + wx * qxx + wm * qxz
                 p_old, q_old = old[0, z, half, rows, :], old[1, z, half, rows, :]
-                amount = dep[j, c, half]
-                cou = coef[0, c, half]
-                new_p = twice_p - p_old + cou * (coef[1, c, half] * horiz + vert_q) + amount
-                new_q = twice_q - q_old + cou * (coef[2, c, half] * horiz + vert_q) + amount
+                amount = dep[j, c, half, inner, :]
+                cou = coef[0, c, half, inner, :]
+                new_p = twice_p - p_old + cou * (coef[1, c, half, inner, :] * horiz + vert_q) + amount
+                new_q = twice_q - q_old + cou * (coef[2, c, half, inner, :] * horiz + vert_q) + amount
                 there[0, z, half, rows, :] = jnp.where(active, new_p, p)
                 there[1, z, half, rows, :] = jnp.where(active, new_q, q)
                 old[0, z, half, rows, :] = jnp.where(active, p, p_old)
@@ -441,7 +448,7 @@
             here, there = there, here
         if here is new:
             for f in range(2):
-                now[f, DEEP : DEEP + nz, :, rows, :] = new[f, DEEP : DEEP + nz, :, rows, :]
+                now[f, DEEP : DEEP + nz, :, block, :] = new[f, DEEP : DEEP + nz, :, block, :]
         return carry
 
     lax.fori_loop(0, SNAPS, window_steps, 0)

time: 35.4 us -> 35 us (0.989)
  Pallas kernels: 32.4 us -> 32 us
    pallas_call x1, Pallas kernels: 32.4 us -> 32 us  [local(): pl.pallas_call(functools.partial(kernel, sizes), out_shape=(jax.ShapeDtyp...]
where the time goes in v1:
time: 35 us; the launch traced here: 34.8 us
  Pallas kernels  32 us (91%)
  local copies, waits for them, and re-layouts  2.19 us (6%)
  between operations  0.64 us (2%)
    pallas_call x1, Pallas kernels, local(): pl.pallas_call(functools.partial(kernel, sizes), out_shape=(jax.ShapeDtyp...  32 us
    unnamed x3, local copies, waits for them, and re-layouts  2.19 us

profile of v1, /device:TPU:0, one launch (start us, length us, event | category | flops | bytes accessed | tf_op | source)
XLA Modules:
  0.0 34.8 jit_solution(8846423783092773258)
XLA Ops:
  0.6 32.0 %shard_map.139 = (bf16[48,64,128]{2,1,0:T(8,128)(2,1)S(1)}, f32[4,8,8,128]{3,2,1,0:T(8,128)S(1)}, f32[4,8,8,128]{3,2,1,0:T(8,128)S(1)}) custom-call(f32[4,8,8,128]{3,2,1,0:T(8,128)} %src_ref.1, f32[4,8,8,128]{3,2,1,0:T(8,128)} %rec_ref.1, f32[8,8,128]{2,1,0:T(8,128)} %cou_ref.1, f32[8,8,128]{2,1,0:T(8,128)} %eps_ref.1, f32[8,8,128]{2,1,0:T(8,128)} %del_ref.1, ...), custom_call_target="tpu_custom_call" | custom-call | tf_op jit(solution)/shard_map/pallas_call | solution.py:520
  32.7 0.9 %copy.18 = bf16[48,8,8,128]{3,2,1,0:T(8,128)(2,1)} copy(bf16[48,8,8,128]{3,2,1,0:T(8,128)(2,1)S(1)} %bitcast.3) | data formatting | bytes 1572864
  33.5 0.7 %copy.19 = f32[4,8,8,128]{3,2,1,0:T(8,128)} copy(f32[4,8,8,128]{3,2,1,0:T(8,128)S(1)} %get-tuple-element.13) | data formatting | bytes 262144
  34.2 0.7 %copy.20 = f32[4,8,8,128]{3,2,1,0:T(8,128)} copy(f32[4,8,8,128]{3,2,1,0:T(8,128)S(1)} %get-tuple-element.14) | data formatting | bytes 262144
